TPU v7x, 32 devices: a whole 2x2x4 slice. The times are simulated.
32 devices in a mesh: dp: 4 (over z), ctx: 8 (over y, x, core).
Axes of the slice: x: 2, y: 2, z: 4, core: 2. Of those that a mesh axis runs over, the one named last changes fastest.
Arguments:
- queries: bfloat16 [8192, 4096], P(('dp', 'ctx')), parts along dimension 0, may hold values from -5 to 5
- keys_values: bfloat16 [8192, 2, 1024], P(('dp', 'ctx')), parts along dimension 0, may hold values from -5 to 5
- fold: int32 [64], P('dp'), parts along dimension 0, may hold values from 0 to 15, each once
- doc_length: int32 [4], P('dp'), parts along dimension 0, may hold values from 1024 to 2048
Outputs:
- attended: bfloat16 [8192, 4096], P(('dp', 'ctx')), parts along dimension 0
There are 4 independent parts, one for each index of `dp`. A program takes and returns all parts, laid end to end along the dimension named above; each array names one. Nothing has to cross between parts.
Inputs may be any that keep to these rules, and one draw needn't show every extreme that they name: A permutation: slot s, the stored rows s * 128 to (s + 1) * 128 - 1, holds positions fold[s] * 128 onwards. `doc_length`: positions at or beyond it are padding.
All inputs are finite; a program needn't handle non-finite values.
Results may differ from a plain program's by a relative error of at most 0.004.
Values may be sent and summed in bfloat16 or wider, within the bound.
No kernel may reach another device: no remote copies, remote signals or barrier semaphores. Data moves between devices by JAX's collectives and lax.ppermute only.
A program may use at most 320 MiB of HBM per device.

v0:
```python
import math

import jax
import jax.numpy as jnp
from jax import lax
from jax.sharding import PartitionSpec as P

HEADS = 32
KV_HEADS = 8
HEAD_DIM = 128


def from_behind(block, axis, distance):
    devices = range(lax.axis_size(axis))
    route = [((i - distance) % len(devices), i) for i in devices]
    return lax.ppermute(block, axis, route)


def shards(queries, keys_values, fold, doc_length):
    cycle_size = lax.axis_size("ctx")
    my_index = lax.axis_index("ctx")
    row_count = queries.shape[0]
    span_rows = row_count // 2
    group_size = HEADS // KV_HEADS
    score_scale = 1.0 / math.sqrt(HEAD_DIM)
    span_ids = jnp.arange(fold.shape[0], dtype=jnp.int32)
    length = doc_length[0]

    def positions(row_ids):
        slot_ids = row_ids // span_rows
        span_of = jnp.sum(
            jnp.where(slot_ids[:, None] == span_ids[None, :], fold[None, :], 0), axis=1
        )
        return span_of * span_rows + row_ids % span_rows

    query_pos = positions(my_index * row_count + jnp.arange(row_count, dtype=jnp.int32))
    query_block = queries.reshape(row_count, KV_HEADS, group_size, HEAD_DIM)

    def absorb(state_now, segment, offset_row):
        block_rows = segment.shape[0]
        key_pos = positions(offset_row + jnp.arange(block_rows, dtype=jnp.int32))
        visible = (key_pos[None, :] <= query_pos[:, None]) & (key_pos < length)[None, :]
        running_max, weight_sum, numerator = state_now
        key_block = segment[:, 0].reshape(block_rows, KV_HEADS, HEAD_DIM)
        value_block = segment[:, 1].reshape(block_rows, KV_HEADS, HEAD_DIM)
        scores = (
            jnp.einsum("qgjd,kgd->qgjk", query_block, key_block, preferred_element_type=jnp.float32)
            * score_scale
        )
        key_mask = visible[:, None, None, :]
        scores = jnp.where(key_mask, scores, -1e30)
        new_max = jnp.maximum(running_max, jnp.max(scores, axis=3))
        weights = jnp.where(key_mask, jnp.exp(scores - new_max[..., None]), 0.0)
        rescale = jnp.exp(running_max - new_max)
        weight_sum = weight_sum * rescale + jnp.sum(weights, axis=3)
        product = jnp.einsum(
            "qgjk,kgd->qgjd",
            weights.astype(jnp.bfloat16),
            value_block,
            preferred_element_type=jnp.float32,
        )
        numerator = numerator * rescale[..., None] + product
        return (new_max, weight_sum, numerator)

    initial = (
        jnp.full((row_count, KV_HEADS, group_size), -1e30, jnp.float32),
        jnp.zeros((row_count, KV_HEADS, group_size), jnp.float32),
        jnp.zeros((row_count, KV_HEADS, group_size, HEAD_DIM), jnp.float32),
    )
    state_now = absorb(initial, keys_values, my_index * row_count)

    def turn(turn_index, carried):
        state_in, travelling = carried
        travelling = from_behind(travelling, "ctx", 1)
        anchor = (my_index - turn_index) % cycle_size
        return (absorb(state_in, travelling, anchor * row_count), travelling)

    state_now, _ = lax.fori_loop(1, cycle_size, turn, (state_now, keys_values))
    _, weight_sum, numerator = state_now
    result = (numerator / weight_sum[..., None]).reshape(row_count, HEADS * HEAD_DIM)
    result = jnp.where((query_pos < length)[:, None], result, 0.0)
    return result.astype(jnp.bfloat16)


def solution(mesh):
    in_specs = (P(("dp", "ctx"), None), P(("dp", "ctx"), None, None), P("dp"), P("dp"))
    out_specs = P(("dp", "ctx"), None)
    return jax.shard_map(shards, mesh=mesh, in_specs=in_specs, out_specs=out_specs, check_vma=False)
```

profile of v0, /device:TPU:12, one launch (start us, length us, event | category | flops | bytes accessed | tf_op | source)
XLA Modules:
  0.0 209.9 jit_solution(13386481054050952217)
XLA Ops:
  1.6 2.4 %copy.24 = bf16[256,2,1024]{0,2,1:T(8,128)(2,1)S(1)} copy(bf16[256,2,1024]{2,1,0:T(2,128)(2,1)} %param.7) | data formatting | bytes 2097152 | tf_op args[1]
  4.9 4.1 %copy.25 = bf16[256,4096]{0,1:T(8,128)(2,1)} copy(bf16[256,4096]{1,0:T(8,128)(2,1)} %param.6) | data formatting | bytes 4194304 | tf_op args[0]
  9.0 3.0 %copy.32 = bf16[256,8,4,128]{3,0,2,1:T(8,128)(2,1)S(1)} copy(bf16[256,8,4,128]{0,3,2,1:T(8,128)(2,1)} %bitcast.96) | data formatting | bytes 4194304
  12.1 3.1 %fusion.19 = (f32[256,8,4]{0,2,1:T(4,128)S(1)}, f32[8,256,256,4]{2,1,3,0:T(8,128)S(1)}) fusion(pred[256,256]{0,1:T(8,128)(4,1)S(1)} %compare_and_fusion.1, bf16[256,8,128,1]{0,2,3,1:T(8,128)(2,1)S(1)} %bitcast.102, bf16[256,8,4,128]{0,3,2,1:T(8,128)(2,1)} %bitcast.97), kind=kOutput, calls=%fused_computation.33 | convolution fusion | flops 543154176 | bytes 11108352 | tf_op jit(solution)/shard_map/qgjd,kgd->qgjk/dot_general | solution.py:47
  15.2 2.1 %fusion.21 = f32[256,8,4]{0,2,1:T(4,128)S(1)} fusion(f32[8,256,256,4]{2,1,3,0:T(8,128)S(1)} %get-tuple-element.389, f32[256,8,4]{0,2,1:T(4,128)S(1)} %broadcast_maximum_fusion, pred[256,256]{0,1:T(8,128)(4,1)S(1)} %compare_and_fusion.1), kind=kLoop, calls=%fused_computation.35 | loop fusion | flops 10477568 | bytes 8519680 | tf_op jit(solution)/shard_map/reduce_sum | solution.py:55
  17.4 4.7 %bitcast_add_fusion.1 = f32[256,8,4,128]{3,0,2,1:T(8,128)} fusion(f32[256,8,4]{0,2,1:T(4,128)S(1)} %get-tuple-element.386, bf16[256,8,128,1]{0,2,3,1:T(8,128)(2,1)S(1)} %bitcast.106, f32[8,256,256,4]{2,1,3,0:T(8,128)S(1)} %get-tuple-element.389, f32[256,8,4]{0,2,1:T(4,128)S(1)} %broadcast_maximum_fusion, pred[256,256]{0,1:T(8,128)(4,1)S(1)} %compare_and_fusion.1), kind=kOutput, calls=%fused_computation.37 | convolution fusion | flops 548405248 | bytes 13238272 | tf_op jit(solution)/shard_map/qgjk,kgd->qgjd/dot_general | solution.py:56
  22.1 176.8 %while.23 = (s32[]{:T(128)}, f32[256,8,4]{0,2,1:T(4,128)S(1)}, f32[256,8,4]{0,2,1:T(4,128)S(1)}, f32[256,8,4,128]{3,0,2,1:T(8,128)}, bf16[256,2,1024]{0,2,1:T(8,...) while((s32[]{:T(128)}, f32[256,8,4]{0,2,1:T(4,128)S(1)}, ...), condition=%wide.region_7.8_spmd.clone, body=%wide.region_3.7_spmd.clone.sunk | while | flops 1103269376 | bytes 79437752 | solution.py:78
  23.0 14.4 %collective-permute-done = bf16[256,2,1024]{0,2,1:T(8,128)(2,1)S(1)} collective-permute-done((bf16[256,2,1024]{0,2,1:T(8,128)(2,1)}, bf16[256,2,1024]{0,2,1:T(8,128)(2,1)S(1)}, u32[]{:S(2)}, u32[]{:S(2)}) %collective-permute-start) | collective-permute-done | bytes 1048608 | tf_op jit(solution)/shard_map/while/body/eval_jaxpr/ppermute | solution.py:16
  37.5 1.5 fusion.59
  39.1 2.2 %fusion.60 = f32[256,8,4]{0,2,1:T(4,128)S(1)} fusion(f32[8,256,256,4]{2,1,3,0:T(8,128)S(1)} %get-tuple-element.467, f32[256,8,4]{0,2,1:T(4,128)S(1)} %max.13, pred[256,256]{0,1:T(8,128)(4,1)S(1)} %compare_and_fusion.3), kind=kLoop, calls=%fused_computation.5.clone.1 | loop fusion | flops 10477568 | bytes 8519680 | tf_op jit(solution)/shard_map/while/body/eval_jaxpr/reduce_sum | solution.py:55
  41.3 3.8 %bitcast_add_fusion.3 = f32[256,8,4,128]{3,0,2,1:T(8,128)S(1)} fusion(f32[256,8,4,128]{3,0,2,1:T(8,128)S(1)} %copy-done, f32[256,8,4]{0,2,1:T(4,128)S(1)} %bitcast.105, bf16[256,8,128,1]{0,2,3,1:T(8,128)(2,1)S(1)} %bitcast.99, f32[8,256,256,4]{2,1,3,0:T(8,128)S(1)} %get-tuple-element.467, f32[256,8,4]{0,2,1:T(4,128)S(1)} %max.13, ...), kind=kOutput, calls=%fused_computation.7.clone.1 | convolution fusion | flops 549453824 | bytes 17432576 | tf_op jit(solution)/shard_map/while/body/eval_jaxpr/qgjk,kgd->qgjd/dot_general | solution.py:56
  45.1 1.0 copy.63
  46.1 1.2 copy-done.1
  48.3 14.4 %collective-permute-done = bf16[256,2,1024]{0,2,1:T(8,128)(2,1)S(1)} collective-permute-done((bf16[256,2,1024]{0,2,1:T(8,128)(2,1)}, bf16[256,2,1024]{0,2,1:T(8,128)(2,1)S(1)}, u32[]{:S(2)}, u32[]{:S(2)}) %collective-permute-start) | collective-permute-done | bytes 1048608 | tf_op jit(solution)/shard_map/while/body/eval_jaxpr/ppermute | solution.py:16
  62.8 1.5 fusion.59
  64.4 2.2 %fusion.60 = f32[256,8,4]{0,2,1:T(4,128)S(1)} fusion(f32[8,256,256,4]{2,1,3,0:T(8,128)S(1)} %get-tuple-element.467, f32[256,8,4]{0,2,1:T(4,128)S(1)} %max.13, pred[256,256]{0,1:T(8,128)(4,1)S(1)} %compare_and_fusion.3), kind=kLoop, calls=%fused_computation.5.clone.1 | loop fusion | flops 10477568 | bytes 8519680 | tf_op jit(solution)/shard_map/while/body/eval_jaxpr/reduce_sum | solution.py:55
  66.6 3.8 %bitcast_add_fusion.3 = f32[256,8,4,128]{3,0,2,1:T(8,128)S(1)} fusion(f32[256,8,4,128]{3,0,2,1:T(8,128)S(1)} %copy-done, f32[256,8,4]{0,2,1:T(4,128)S(1)} %bitcast.105, bf16[256,8,128,1]{0,2,3,1:T(8,128)(2,1)S(1)} %bitcast.99, f32[8,256,256,4]{2,1,3,0:T(8,128)S(1)} %get-tuple-element.467, f32[256,8,4]{0,2,1:T(4,128)S(1)} %max.13, ...), kind=kOutput, calls=%fused_computation.7.clone.1 | convolution fusion | flops 549453824 | bytes 17432576 | tf_op jit(solution)/shard_map/while/body/eval_jaxpr/qgjk,kgd->qgjd/dot_general | solution.py:56
  70.4 1.0 copy.63
  71.4 1.2 copy-done.1
  73.5 14.4 %collective-permute-done = bf16[256,2,1024]{0,2,1:T(8,128)(2,1)S(1)} collective-permute-done((bf16[256,2,1024]{0,2,1:T(8,128)(2,1)}, bf16[256,2,1024]{0,2,1:T(8,128)(2,1)S(1)}, u32[]{:S(2)}, u32[]{:S(2)}) %collective-permute-start) | collective-permute-done | bytes 1048608 | tf_op jit(solution)/shard_map/while/body/eval_jaxpr/ppermute | solution.py:16
  88.0 1.5 fusion.59
  89.6 2.2 %fusion.60 = f32[256,8,4]{0,2,1:T(4,128)S(1)} fusion(f32[8,256,256,4]{2,1,3,0:T(8,128)S(1)} %get-tuple-element.467, f32[256,8,4]{0,2,1:T(4,128)S(1)} %max.13, pred[256,256]{0,1:T(8,128)(4,1)S(1)} %compare_and_fusion.3), kind=kLoop, calls=%fused_computation.5.clone.1 | loop fusion | flops 10477568 | bytes 8519680 | tf_op jit(solution)/shard_map/while/body/eval_jaxpr/reduce_sum | solution.py:55
  91.8 3.8 %bitcast_add_fusion.3 = f32[256,8,4,128]{3,0,2,1:T(8,128)S(1)} fusion(f32[256,8,4,128]{3,0,2,1:T(8,128)S(1)} %copy-done, f32[256,8,4]{0,2,1:T(4,128)S(1)} %bitcast.105, bf16[256,8,128,1]{0,2,3,1:T(8,128)(2,1)S(1)} %bitcast.99, f32[8,256,256,4]{2,1,3,0:T(8,128)S(1)} %get-tuple-element.467, f32[256,8,4]{0,2,1:T(4,128)S(1)} %max.13, ...), kind=kOutput, calls=%fused_computation.7.clone.1 | convolution fusion | flops 549453824 | bytes 17432576 | tf_op jit(solution)/shard_map/while/body/eval_jaxpr/qgjk,kgd->qgjd/dot_general | solution.py:56
  96.7 1.2 copy-done.1
  98.8 14.4 %collective-permute-done = bf16[256,2,1024]{0,2,1:T(8,128)(2,1)S(1)} collective-permute-done((bf16[256,2,1024]{0,2,1:T(8,128)(2,1)}, bf16[256,2,1024]{0,2,1:T(8,128)(2,1)S(1)}, u32[]{:S(2)}, u32[]{:S(2)}) %collective-permute-start) | collective-permute-done | bytes 1048608 | tf_op jit(solution)/shard_map/while/body/eval_jaxpr/ppermute | solution.py:16
  113.3 1.5 fusion.59
  114.9 2.2 %fusion.60 = f32[256,8,4]{0,2,1:T(4,128)S(1)} fusion(f32[8,256,256,4]{2,1,3,0:T(8,128)S(1)} %get-tuple-element.467, f32[256,8,4]{0,2,1:T(4,128)S(1)} %max.13, pred[256,256]{0,1:T(8,128)(4,1)S(1)} %compare_and_fusion.3), kind=kLoop, calls=%fused_computation.5.clone.1 | loop fusion | flops 10477568 | bytes 8519680 | tf_op jit(solution)/shard_map/while/body/eval_jaxpr/reduce_sum | solution.py:55
  117.1 3.8 %bitcast_add_fusion.3 = f32[256,8,4,128]{3,0,2,1:T(8,128)S(1)} fusion(f32[256,8,4,128]{3,0,2,1:T(8,128)S(1)} %copy-done, f32[256,8,4]{0,2,1:T(4,128)S(1)} %bitcast.105, bf16[256,8,128,1]{0,2,3,1:T(8,128)(2,1)S(1)} %bitcast.99, f32[8,256,256,4]{2,1,3,0:T(8,128)S(1)} %get-tuple-element.467, f32[256,8,4]{0,2,1:T(4,128)S(1)} %max.13, ...), kind=kOutput, calls=%fused_computation.7.clone.1 | convolution fusion | flops 549453824 | bytes 17432576 | tf_op jit(solution)/shard_map/while/body/eval_jaxpr/qgjk,kgd->qgjd/dot_general | solution.py:56
  121.9 1.2 copy-done.1
  124.1 14.4 %collective-permute-done = bf16[256,2,1024]{0,2,1:T(8,128)(2,1)S(1)} collective-permute-done((bf16[256,2,1024]{0,2,1:T(8,128)(2,1)}, bf16[256,2,1024]{0,2,1:T(8,128)(2,1)S(1)}, u32[]{:S(2)}, u32[]{:S(2)}) %collective-permute-start) | collective-permute-done | bytes 1048608 | tf_op jit(solution)/shard_map/while/body/eval_jaxpr/ppermute | solution.py:16
  138.6 1.5 fusion.59
  140.1 2.2 %fusion.60 = f32[256,8,4]{0,2,1:T(4,128)S(1)} fusion(f32[8,256,256,4]{2,1,3,0:T(8,128)S(1)} %get-tuple-element.467, f32[256,8,4]{0,2,1:T(4,128)S(1)} %max.13, pred[256,256]{0,1:T(8,128)(4,1)S(1)} %compare_and_fusion.3), kind=kLoop, calls=%fused_computation.5.clone.1 | loop fusion | flops 10477568 | bytes 8519680 | tf_op jit(solution)/shard_map/while/body/eval_jaxpr/reduce_sum | solution.py:55
  142.3 3.8 %bitcast_add_fusion.3 = f32[256,8,4,128]{3,0,2,1:T(8,128)S(1)} fusion(f32[256,8,4,128]{3,0,2,1:T(8,128)S(1)} %copy-done, f32[256,8,4]{0,2,1:T(4,128)S(1)} %bitcast.105, bf16[256,8,128,1]{0,2,3,1:T(8,128)(2,1)S(1)} %bitcast.99, f32[8,256,256,4]{2,1,3,0:T(8,128)S(1)} %get-tuple-element.467, f32[256,8,4]{0,2,1:T(4,128)S(1)} %max.13, ...), kind=kOutput, calls=%fused_computation.7.clone.1 | convolution fusion | flops 549453824 | bytes 17432576 | tf_op jit(solution)/shard_map/while/body/eval_jaxpr/qgjk,kgd->qgjd/dot_general | solution.py:56
  147.2 1.2 copy-done.1
  149.3 14.4 %collective-permute-done = bf16[256,2,1024]{0,2,1:T(8,128)(2,1)S(1)} collective-permute-done((bf16[256,2,1024]{0,2,1:T(8,128)(2,1)}, bf16[256,2,1024]{0,2,1:T(8,128)(2,1)S(1)}, u32[]{:S(2)}, u32[]{:S(2)}) %collective-permute-start) | collective-permute-done | bytes 1048608 | tf_op jit(solution)/shard_map/while/body/eval_jaxpr/ppermute | solution.py:16
  163.8 1.5 fusion.59
  165.4 2.2 %fusion.60 = f32[256,8,4]{0,2,1:T(4,128)S(1)} fusion(f32[8,256,256,4]{2,1,3,0:T(8,128)S(1)} %get-tuple-element.467, f32[256,8,4]{0,2,1:T(4,128)S(1)} %max.13, pred[256,256]{0,1:T(8,128)(4,1)S(1)} %compare_and_fusion.3), kind=kLoop, calls=%fused_computation.5.clone.1 | loop fusion | flops 10477568 | bytes 8519680 | tf_op jit(solution)/shard_map/while/body/eval_jaxpr/reduce_sum | solution.py:55
  167.6 3.8 %bitcast_add_fusion.3 = f32[256,8,4,128]{3,0,2,1:T(8,128)S(1)} fusion(f32[256,8,4,128]{3,0,2,1:T(8,128)S(1)} %copy-done, f32[256,8,4]{0,2,1:T(4,128)S(1)} %bitcast.105, bf16[256,8,128,1]{0,2,3,1:T(8,128)(2,1)S(1)} %bitcast.99, f32[8,256,256,4]{2,1,3,0:T(8,128)S(1)} %get-tuple-element.467, f32[256,8,4]{0,2,1:T(4,128)S(1)} %max.13, ...), kind=kOutput, calls=%fused_computation.7.clone.1 | convolution fusion | flops 549453824 | bytes 17432576 | tf_op jit(solution)/shard_map/while/body/eval_jaxpr/qgjk,kgd->qgjd/dot_general | solution.py:56
  172.4 1.2 copy-done.1
  174.6 14.4 %collective-permute-done = bf16[256,2,1024]{0,2,1:T(8,128)(2,1)S(1)} collective-permute-done((bf16[256,2,1024]{0,2,1:T(8,128)(2,1)}, bf16[256,2,1024]{0,2,1:T(8,128)(2,1)S(1)}, u32[]{:S(2)}, u32[]{:S(2)}) %collective-permute-start) | collective-permute-done | bytes 1048608 | tf_op jit(solution)/shard_map/while/body/eval_jaxpr/ppermute | solution.py:16
  189.1 1.5 fusion.59
  190.7 2.2 %fusion.60 = f32[256,8,4]{0,2,1:T(4,128)S(1)} fusion(f32[8,256,256,4]{2,1,3,0:T(8,128)S(1)} %get-tuple-element.467, f32[256,8,4]{0,2,1:T(4,128)S(1)} %max.13, pred[256,256]{0,1:T(8,128)(4,1)S(1)} %compare_and_fusion.3), kind=kLoop, calls=%fused_computation.5.clone.1 | loop fusion | flops 10477568 | bytes 8519680 | tf_op jit(solution)/shard_map/while/body/eval_jaxpr/reduce_sum | solution.py:55
  192.9 3.8 %bitcast_add_fusion.3 = f32[256,8,4,128]{3,0,2,1:T(8,128)S(1)} fusion(f32[256,8,4,128]{3,0,2,1:T(8,128)S(1)} %copy-done, f32[256,8,4]{0,2,1:T(4,128)S(1)} %bitcast.105, bf16[256,8,128,1]{0,2,3,1:T(8,128)(2,1)S(1)} %bitcast.99, f32[8,256,256,4]{2,1,3,0:T(8,128)S(1)} %get-tuple-element.467, f32[256,8,4]{0,2,1:T(4,128)S(1)} %max.13, ...), kind=kOutput, calls=%fused_computation.7.clone.1 | convolution fusion | flops 549453824 | bytes 17432576 | tf_op jit(solution)/shard_map/while/body/eval_jaxpr/qgjk,kgd->qgjd/dot_general | solution.py:56
  197.7 1.2 copy-done.1
  198.9 2.9 %broadcast_divide_fusion = bf16[256,8,4,128]{3,0,2,1:T(8,128)(2,1)S(1)} fusion(f32[256,8,4,128]{3,0,2,1:T(8,128)} %get-tuple-element.310, f32[256,8,4]{0,2,1:T(4,128)S(1)} %get-tuple-element.311), kind=kLoop, calls=%fused_computation.44 | loop fusion | flops 2097152 | bytes 6324224 | tf_op jit(solution)/shard_map/div | solution.py:80
  201.8 2.9 %copy.33 = bf16[256,8,4,128]{3,2,1,0:T(4,128)(2,1)} copy(bf16[256,8,4,128]{3,0,2,1:T(8,128)(2,1)S(1)} %broadcast_divide_fusion) | data formatting | bytes 4194304 | tf_op jit(solution)/shard_map/div | solution.py:80
  204.7 3.3 %reshape.205 = bf16[256,4096]{1,0:T(8,128)(2,1)S(1)} reshape(bf16[256,8,4,128]{3,2,1,0:T(4,128)(2,1)} %copy.33) | data formatting | bytes 4194304 | tf_op jit(solution)/shard_map/reshape | solution.py:80
  208.0 1.9 select_convert_fusion
  (102 shorter events, 14.0 us)
Async XLA Ops:
  4.0 5.0 %copy-start.2 = (bf16[256,2,1024]{0,2,1:T(8,128)(2,1)}, bf16[256,2,1024]{0,2,1:T(8,128)(2,1)S(1)}, u32[]{:S(2)}) copy-start(bf16[256,2,1024]{0,2,1:T(8,128)(2,1)S(1)} %copy.24) | copy-start | bytes 3145732
  12.0 5.4 %copy-start.3 = (bf16[256,1,1024]{0,2,1:T(8,128)(2,1)S(1)}, bf16[256,1,1024]{0,2,1:T(8,128)(2,1)}, u32[]{:S(2)}) copy-start(bf16[256,1,1024]{0,2,1:T(8,128)(2,1)} %get-tuple-element.384) | copy-start | bytes 1572868
  17.4 4.7 %copy-start.4 = (s32[16]{0:T(128)S(1)}, s32[16]{0:T(128)}, u32[]{:S(2)}) copy-start(s32[16]{0:T(128)} %param.8) | copy-start | bytes 196
  22.1 15.3 %collective-permute-start = (bf16[256,2,1024]{0,2,1:T(8,128)(2,1)}, bf16[256,2,1024]{0,2,1:T(8,128)(2,1)S(1)}, u32[]{:S(2)}, u32[]{:S(2)}) collective-permute-start(bf16[256,2,1024]{0,2,1:T(8,128)(2,1)} %get-tuple-element.490), channel_id=1, source_target_pairs={{7,0},{0,1},{1,2},{2,3},{3,4},{4,5},{5,6},{6,7},{15,8},{8,9},{9,10... | collective-permute-start | bytes 3145736 | tf_op jit(solution)/shard_map/while/body/eval_jaxpr/ppermute | solution.py:16
  37.5 3.8 %copy-start = (f32[256,8,4,128]{3,0,2,1:T(8,128)S(1)}, f32[256,8,4,128]{3,0,2,1:T(8,128)}, u32[]{:S(2)}) copy-start(f32[256,8,4,128]{3,0,2,1:T(8,128)} %get-tuple-element.489) | copy-start | bytes 12582916 | tf_op jit(solution)/shard_map/while
  45.1 2.2 %copy-start.1 = (f32[256,8,4,128]{3,0,2,1:T(8,128)}, f32[256,8,4,128]{3,0,2,1:T(8,128)S(1)}, u32[]{:S(2)}) copy-start(f32[256,8,4,128]{3,0,2,1:T(8,128)S(1)} %bitcast_add_fusion.3) | copy-start | bytes 12582916 | tf_op jit(solution)/shard_map/while
  47.4 15.3 %collective-permute-start = (bf16[256,2,1024]{0,2,1:T(8,128)(2,1)}, bf16[256,2,1024]{0,2,1:T(8,128)(2,1)S(1)}, u32[]{:S(2)}, u32[]{:S(2)}) collective-permute-start(bf16[256,2,1024]{0,2,1:T(8,128)(2,1)} %get-tuple-element.490), channel_id=1, source_target_pairs={{7,0},{0,1},{1,2},{2,3},{3,4},{4,5},{5,6},{6,7},{15,8},{8,9},{9,10... | collective-permute-start | bytes 3145736 | tf_op jit(solution)/shard_map/while/body/eval_jaxpr/ppermute | solution.py:16
  62.8 3.8 %copy-start = (f32[256,8,4,128]{3,0,2,1:T(8,128)S(1)}, f32[256,8,4,128]{3,0,2,1:T(8,128)}, u32[]{:S(2)}) copy-start(f32[256,8,4,128]{3,0,2,1:T(8,128)} %get-tuple-element.489) | copy-start | bytes 12582916 | tf_op jit(solution)/shard_map/while
  70.4 2.2 %copy-start.1 = (f32[256,8,4,128]{3,0,2,1:T(8,128)}, f32[256,8,4,128]{3,0,2,1:T(8,128)S(1)}, u32[]{:S(2)}) copy-start(f32[256,8,4,128]{3,0,2,1:T(8,128)S(1)} %bitcast_add_fusion.3) | copy-start | bytes 12582916 | tf_op jit(solution)/shard_map/while
  72.6 15.3 %collective-permute-start = (bf16[256,2,1024]{0,2,1:T(8,128)(2,1)}, bf16[256,2,1024]{0,2,1:T(8,128)(2,1)S(1)}, u32[]{:S(2)}, u32[]{:S(2)}) collective-permute-start(bf16[256,2,1024]{0,2,1:T(8,128)(2,1)} %get-tuple-element.490), channel_id=1, source_target_pairs={{7,0},{0,1},{1,2},{2,3},{3,4},{4,5},{5,6},{6,7},{15,8},{8,9},{9,10... | collective-permute-start | bytes 3145736 | tf_op jit(solution)/shard_map/while/body/eval_jaxpr/ppermute | solution.py:16
  88.0 3.8 %copy-start = (f32[256,8,4,128]{3,0,2,1:T(8,128)S(1)}, f32[256,8,4,128]{3,0,2,1:T(8,128)}, u32[]{:S(2)}) copy-start(f32[256,8,4,128]{3,0,2,1:T(8,128)} %get-tuple-element.489) | copy-start | bytes 12582916 | tf_op jit(solution)/shard_map/while
  95.6 2.2 %copy-start.1 = (f32[256,8,4,128]{3,0,2,1:T(8,128)}, f32[256,8,4,128]{3,0,2,1:T(8,128)S(1)}, u32[]{:S(2)}) copy-start(f32[256,8,4,128]{3,0,2,1:T(8,128)S(1)} %bitcast_add_fusion.3) | copy-start | bytes 12582916 | tf_op jit(solution)/shard_map/while
  97.9 15.3 %collective-permute-start = (bf16[256,2,1024]{0,2,1:T(8,128)(2,1)}, bf16[256,2,1024]{0,2,1:T(8,128)(2,1)S(1)}, u32[]{:S(2)}, u32[]{:S(2)}) collective-permute-start(bf16[256,2,1024]{0,2,1:T(8,128)(2,1)} %get-tuple-element.490), channel_id=1, source_target_pairs={{7,0},{0,1},{1,2},{2,3},{3,4},{4,5},{5,6},{6,7},{15,8},{8,9},{9,10... | collective-permute-start | bytes 3145736 | tf_op jit(solution)/shard_map/while/body/eval_jaxpr/ppermute | solution.py:16
  113.3 3.8 %copy-start = (f32[256,8,4,128]{3,0,2,1:T(8,128)S(1)}, f32[256,8,4,128]{3,0,2,1:T(8,128)}, u32[]{:S(2)}) copy-start(f32[256,8,4,128]{3,0,2,1:T(8,128)} %get-tuple-element.489) | copy-start | bytes 12582916 | tf_op jit(solution)/shard_map/while
  120.9 2.2 %copy-start.1 = (f32[256,8,4,128]{3,0,2,1:T(8,128)}, f32[256,8,4,128]{3,0,2,1:T(8,128)S(1)}, u32[]{:S(2)}) copy-start(f32[256,8,4,128]{3,0,2,1:T(8,128)S(1)} %bitcast_add_fusion.3) | copy-start | bytes 12582916 | tf_op jit(solution)/shard_map/while
  123.1 15.3 %collective-permute-start = (bf16[256,2,1024]{0,2,1:T(8,128)(2,1)}, bf16[256,2,1024]{0,2,1:T(8,128)(2,1)S(1)}, u32[]{:S(2)}, u32[]{:S(2)}) collective-permute-start(bf16[256,2,1024]{0,2,1:T(8,128)(2,1)} %get-tuple-element.490), channel_id=1, source_target_pairs={{7,0},{0,1},{1,2},{2,3},{3,4},{4,5},{5,6},{6,7},{15,8},{8,9},{9,10... | collective-permute-start | bytes 3145736 | tf_op jit(solution)/shard_map/while/body/eval_jaxpr/ppermute | solution.py:16
  138.6 3.8 %copy-start = (f32[256,8,4,128]{3,0,2,1:T(8,128)S(1)}, f32[256,8,4,128]{3,0,2,1:T(8,128)}, u32[]{:S(2)}) copy-start(f32[256,8,4,128]{3,0,2,1:T(8,128)} %get-tuple-element.489) | copy-start | bytes 12582916 | tf_op jit(solution)/shard_map/while
  146.2 2.2 %copy-start.1 = (f32[256,8,4,128]{3,0,2,1:T(8,128)}, f32[256,8,4,128]{3,0,2,1:T(8,128)S(1)}, u32[]{:S(2)}) copy-start(f32[256,8,4,128]{3,0,2,1:T(8,128)S(1)} %bitcast_add_fusion.3) | copy-start | bytes 12582916 | tf_op jit(solution)/shard_map/while
  148.4 15.3 %collective-permute-start = (bf16[256,2,1024]{0,2,1:T(8,128)(2,1)}, bf16[256,2,1024]{0,2,1:T(8,128)(2,1)S(1)}, u32[]{:S(2)}, u32[]{:S(2)}) collective-permute-start(bf16[256,2,1024]{0,2,1:T(8,128)(2,1)} %get-tuple-element.490), channel_id=1, source_target_pairs={{7,0},{0,1},{1,2},{2,3},{3,4},{4,5},{5,6},{6,7},{15,8},{8,9},{9,10... | collective-permute-start | bytes 3145736 | tf_op jit(solution)/shard_map/while/body/eval_jaxpr/ppermute | solution.py:16
  163.8 3.8 %copy-start = (f32[256,8,4,128]{3,0,2,1:T(8,128)S(1)}, f32[256,8,4,128]{3,0,2,1:T(8,128)}, u32[]{:S(2)}) copy-start(f32[256,8,4,128]{3,0,2,1:T(8,128)} %get-tuple-element.489) | copy-start | bytes 12582916 | tf_op jit(solution)/shard_map/while
  171.4 2.2 %copy-start.1 = (f32[256,8,4,128]{3,0,2,1:T(8,128)}, f32[256,8,4,128]{3,0,2,1:T(8,128)S(1)}, u32[]{:S(2)}) copy-start(f32[256,8,4,128]{3,0,2,1:T(8,128)S(1)} %bitcast_add_fusion.3) | copy-start | bytes 12582916 | tf_op jit(solution)/shard_map/while
  173.7 15.3 %collective-permute-start = (bf16[256,2,1024]{0,2,1:T(8,128)(2,1)}, bf16[256,2,1024]{0,2,1:T(8,128)(2,1)S(1)}, u32[]{:S(2)}, u32[]{:S(2)}) collective-permute-start(bf16[256,2,1024]{0,2,1:T(8,128)(2,1)} %get-tuple-element.490), channel_id=1, source_target_pairs={{7,0},{0,1},{1,2},{2,3},{3,4},{4,5},{5,6},{6,7},{15,8},{8,9},{9,10... | collective-permute-start | bytes 3145736 | tf_op jit(solution)/shard_map/while/body/eval_jaxpr/ppermute | solution.py:16
  189.1 3.8 %copy-start = (f32[256,8,4,128]{3,0,2,1:T(8,128)S(1)}, f32[256,8,4,128]{3,0,2,1:T(8,128)}, u32[]{:S(2)}) copy-start(f32[256,8,4,128]{3,0,2,1:T(8,128)} %get-tuple-element.489) | copy-start | bytes 12582916 | tf_op jit(solution)/shard_map/while
  196.7 2.2 %copy-start.1 = (f32[256,8,4,128]{3,0,2,1:T(8,128)}, f32[256,8,4,128]{3,0,2,1:T(8,128)S(1)}, u32[]{:S(2)}) copy-start(f32[256,8,4,128]{3,0,2,1:T(8,128)S(1)} %bitcast_add_fusion.3) | copy-start | bytes 12582916 | tf_op jit(solution)/shard_map/while
where the time goes:
time: 211 us; the launch traced here: 210 us
  waiting for transfers between devices  101 us (48%)
  matrix products  45.3 us (21%)
  local copies, waits for them, and re-layouts  32.8 us (16%)
  other arithmetic  29.4 us (14%)
    ppermute x7, waiting for transfers between devices, from_behind(): return lax.ppermute(block, axis, route)  101 us
    dot_general x8, matrix products, absorb(): jnp.einsum('qgjk,kgd->qgjd', weights.astype(jnp.bfloat16), value_block, p...  31.4 us
    reduce_sum x8, other arithmetic, absorb(): weight_sum = weight_sum * rescale + jnp.sum(weights, axis=3)  17.2 us
    while x42, local copies, waits for them, and re-layouts  15.7 us
    dot_general x8, matrix products, absorb(): jnp.einsum('qgjd,kgd->qgjk', query_block, key_block, preferred_element_ty...  14 us
    unnamed x9, local copies, waits for them, and re-layouts  9.53 us
    lt x7, other arithmetic, absorb(): key_pos < length  4.61 us
  transfers between devices with their start and end apart: 7, of which 7 were waited for; matrix products, arithmetic and copies ran while one was open for 3% of the time, Pallas kernels for 0%

commit v1 on v0

v1 whole, which is shorter than its diff:
```python
import functools
import math

import jax
import jax.numpy as jnp
from jax import lax
from jax.experimental import pallas as pl
from jax.experimental.pallas import tpu as pltpu
from jax.sharding import PartitionSpec as P

HEADS = 32
KV_HEADS = 8
HEAD_DIM = 128
GROUP = HEADS // KV_HEADS
HEADS_AT_ONCE = 4
SCALE = math.log2(math.e) / math.sqrt(HEAD_DIM)
LOW, HIGH = 2.0**-90, 2.0**90
NT = (((1,), (1,)), ((), ()))


class Span:
    def __init__(self, pack, index, offset, core, later):
        self.pack, self.index, self.offset, self.core, self.later = pack, index, offset, core, later

    def place(self, table, spans):
        me = table[spans + 1]
        odd = me % 2
        offset = self.offset[0] + odd * (self.offset[1] - self.offset[0])
        core = self.core[0] + odd * (self.core[1] - self.core[0])
        device = ((me - odd) ^ offset) + core
        first, second = table[2 * device], table[2 * device + 1]
        return jnp.maximum(first, second) if self.later else jnp.minimum(first, second)


def stage(held, everything, n_packs, spans, is_first, is_last, *refs):
    refs = list(refs)
    table, q_ref = refs[:2]
    packs = refs[2 : 2 + n_packs]
    rest = refs[2 + n_packs :]
    if not is_first:
        before, rest = rest[0], rest[1:]
    if is_last:
        every = rest[: len({s.pack for s in everything})]
        rest = rest[len(every) :]
        out_hbm, key_buf, value_buf, out_ref, flag, keys_all, values_all, out_sems, sem = rest
        flag[...] = jnp.zeros_like(flag)
    else:
        total, key_buf, value_buf = rest
    span_rows = q_ref.shape[0] // 2
    group_rows = GROUP * span_rows
    me = table[spans + 1]
    length = table[spans]
    count = len(held)

    places = [s.place(table, spans) for s in held]
    for s, place in zip(held, places):
        rank = sum((other < place).astype(jnp.int32) for other in places)
        at = pl.ds(pl.multiple_of(rank * span_rows, span_rows), span_rows)
        key_buf[at, :] = packs[s.pack][s.index, 0]
        value_buf[at, :] = packs[s.pack][s.index, 1]

    def column(head):
        return pl.ds(pl.multiple_of(head * HEAD_DIM, HEAD_DIM), HEAD_DIM)

    def rows_of(i):
        return pl.ds(pl.multiple_of(i * span_rows, span_rows), span_rows)

    def row_in_span():
        return lax.broadcasted_iota(jnp.int32, (group_rows, 1), 0) % span_rows

    def finish(i, g, place, sums):
        real = place * span_rows + row_in_span() < length
        weight_sum = sums[:, HEAD_DIM:]
        value = jnp.where(real, sums[:, :HEAD_DIM] / weight_sum, 0.0).astype(jnp.bfloat16)
        for n in range(GROUP):
            out_ref[rows_of(i), column(g * GROUP + n)] = value[n * span_rows : (n + 1) * span_rows]
        fine = (weight_sum > LOW) & (weight_sum < HIGH) | jnp.logical_not(real)
        flag[...] = jnp.where(fine, flag[...], 1.0)

    def add(i, place, seen):
        if is_first:
            col = lax.broadcasted_iota(jnp.int32, (group_rows, span_rows), 1)
            mask = col <= jnp.minimum(row_in_span(), length - 1 - place * span_rows)

        def some_heads(step, carry):
            for h in range(HEADS_AT_ONCE):
                g = step * HEADS_AT_ONCE + h
                if seen:
                    query = jnp.concatenate([q_ref[rows_of(i), column(g * GROUP + n)] for n in range(GROUP)], axis=0)
                    scores = lax.dot_general(
                        query, key_buf[: seen * span_rows, column(g)], NT, preferred_element_type=jnp.float32
                    )
                    weights = jnp.exp2(scores * SCALE)
                    if is_first:
                        own = jnp.where(mask, weights[:, (seen - 1) * span_rows :], 0.0)
                        parts = [weights[:, : (seen - 1) * span_rows], own]
                        weights = jnp.concatenate(parts, axis=1) if seen > 1 else own
                    ones = jnp.ones((seen * span_rows, HEAD_DIM), jnp.bfloat16)
                    values = jnp.concatenate([value_buf[: seen * span_rows, column(g)], ones], axis=1)
                    product = jnp.dot(weights.astype(jnp.bfloat16), values, preferred_element_type=jnp.float32)
                if is_first:
                    total[i, g] = product
                elif not is_last:
                    total[i, g] = before[i, g] + product
                else:
                    finish(i, g, place, before[i, g] + product if seen else before[i, g])
            return carry

        lax.fori_loop(0, KV_HEADS // HEADS_AT_ONCE, some_heads, 0)

    def one_span(i, carry):
        place = table[2 * me + i]
        seen = sum((other <= place).astype(jnp.int32) for other in places)
        seen = jnp.where(place * span_rows < length, seen, 0)

        for n in range(0 if is_last else 1, count + 1):

            @pl.when(seen == n)
            def _():
                add(i, place, n)

        if is_last:
            pltpu.make_async_copy(out_ref.at[rows_of(i)], out_hbm.at[rows_of(i)], out_sems.at[i]).start()
        return carry

    lax.fori_loop(0, 2, one_span, 0)
    if not is_last:
        return

    for i in range(2):
        pltpu.make_async_copy(out_ref.at[rows_of(i)], out_hbm.at[rows_of(i)], out_sems.at[i]).wait()

    @pl.when(jnp.max(flag[...]) > 0.0)
    def _():
        block = 4 * span_rows

        def one_head(g, carry):
            for s in everything:
                at = pl.ds(pl.multiple_of(s.place(table, spans) * span_rows, span_rows), span_rows)
                for kind, target in enumerate((keys_all, values_all)):
                    copy = pltpu.make_async_copy(every[s.pack].at[s.index, kind, :, column(g)], target.at[at, :], sem)
                    copy.start()
                    copy.wait()

            def one(step, carry):
                i, n = step // GROUP, step % GROUP
                place = table[2 * me + i]
                rows = pl.ds(pl.multiple_of(i * span_rows, span_rows), span_rows)
                query = q_ref[rows, column(g * GROUP + n)]
                row = place * span_rows + lax.broadcasted_iota(jnp.int32, (span_rows, 1), 0)

                def masked(k):
                    at = pl.ds(pl.multiple_of(k * block, block), block)
                    raw = SCALE * lax.dot_general(query, keys_all[at, :], NT, preferred_element_type=jnp.float32)
                    key_pos = k * block + lax.broadcasted_iota(jnp.int32, (span_rows, block), 1)
                    return raw, key_pos <= jnp.minimum(row, length - 1), at

                def top(k, peak):
                    raw, mask, _ = masked(k)
                    return jnp.maximum(peak, jnp.max(jnp.where(mask, raw, -1e30), axis=1, keepdims=True))

                blocks = place // 4 + 1
                peak = lax.fori_loop(0, blocks, top, jnp.full((span_rows, 1), -1e30, jnp.float32))

                def more(k, sums):
                    raw, mask, at = masked(k)
                    weights = jnp.where(mask, jnp.exp2(raw - peak), 0.0)
                    product = jnp.dot(weights.astype(jnp.bfloat16), values_all[at, :], preferred_element_type=jnp.float32)
                    return sums[0] + product, sums[1] + jnp.sum(weights, axis=1, keepdims=True)

                zero = (jnp.zeros((span_rows, HEAD_DIM), jnp.float32), jnp.zeros((span_rows, 1), jnp.float32))
                numerator, weight_sum = lax.fori_loop(0, blocks, more, zero)
                value = jnp.where(row < length, numerator / weight_sum, 0.0)
                out_ref[rows, column(g * GROUP + n)] = value.astype(jnp.bfloat16)
                return carry

            return lax.fori_loop(0, 2 * GROUP, one, carry)

        lax.fori_loop(0, KV_HEADS, one_head, 0)
        copy = pltpu.make_async_copy(out_ref, out_hbm, sem)
        copy.start()
        copy.wait()


def run_stage(table, queries, packs, before, held, everything, spans, is_last, all_packs):
    rows = queries.shape[0]
    span_rows = rows // 2
    vmem = pl.BlockSpec(memory_space=pltpu.VMEM)
    hbm = pl.BlockSpec(memory_space=pl.ANY)
    names = sorted({s.pack for s in held})
    held = [Span(names.index(s.pack), s.index, s.offset, s.core, s.later) for s in held]
    operands = [table, queries] + [packs[n] for n in names]
    specs = [pl.BlockSpec(memory_space=pltpu.SMEM), vmem] + [vmem] * len(names)
    sums = (2, KV_HEADS, GROUP * span_rows, 2 * HEAD_DIM)
    keys = len(held) * span_rows
    scratch = [
        pltpu.VMEM((keys, KV_HEADS * HEAD_DIM), jnp.bfloat16),
        pltpu.VMEM((keys, KV_HEADS * HEAD_DIM), jnp.bfloat16),
    ]
    aliases = {}
    if before is not None:
        operands.append(before)
        specs.append(vmem)
    if is_last:
        operands += all_packs
        specs += [hbm] * len(all_packs)
        out_shape = jax.ShapeDtypeStruct(queries.shape, jnp.bfloat16)
        scratch += [
            pltpu.VMEM(queries.shape, jnp.bfloat16),
            pltpu.VMEM((GROUP * span_rows, HEAD_DIM), jnp.float32),
            pltpu.VMEM((spans * span_rows, HEAD_DIM), jnp.bfloat16),
            pltpu.VMEM((spans * span_rows, HEAD_DIM), jnp.bfloat16),
            pltpu.SemaphoreType.DMA((2,)),
            pltpu.SemaphoreType.DMA,
        ]
    else:
        out_shape = jax.ShapeDtypeStruct(sums, jnp.float32)
        if before is not None:
            aliases = {len(operands) - 1: 0}
    return pl.pallas_call(
        functools.partial(stage, held, everything, len(names), spans, before is None, is_last),
        out_shape=out_shape,
        in_specs=specs,
        out_specs=hbm if is_last else vmem,
        scratch_shapes=scratch,
        input_output_aliases=aliases,
        compiler_params=pltpu.CompilerParams(vmem_limit_bytes=24 << 20),
        cost_estimate=pl.CostEstimate(
            flops=rows * HEADS * keys * HEAD_DIM * 4, bytes_accessed=8 * keys * KV_HEADS * HEAD_DIM, transcendentals=0
        ),
        name="stage",
    )(*operands)


def shards(queries, keys_values, fold, doc_length):
    size = lax.axis_size("ctx")
    me = lax.axis_index("ctx")
    core = me % 2
    rows = queries.shape[0]
    spans = fold.shape[0]
    table = jnp.concatenate([fold, doc_length, me[None].astype(jnp.int32)])

    def swap(block, mask=1):
        return lax.ppermute(block, "ctx", [(i, i ^ mask) for i in range(size)])

    def both_links(block):
        return lax.ppermute(block, "ctx", [(i, i ^ (3 if i % 2 == 0 else 5)) for i in range(size)])

    halves = fold.reshape(size, 2)
    turned = jnp.sum(jnp.where(jnp.arange(size) == me, halves[:, 0] > halves[:, 1], False).astype(jnp.int32))
    half = rows // 2

    def span(start):
        return lax.dynamic_slice_in_dim(keys_values, start, half).transpose(1, 0, 2)[None]

    low, high = span(turned * half), span((1 - turned) * half)

    packs, held = [], []

    def hold(block, offset, cores, later):
        packs.append(block)
        held.append(Span(len(packs) - 1, 0, offset, cores, later))
        return len(packs) - 1

    def run(names, sums, is_last=False):
        return run_stage(table, queries, packs, sums, [s for s in held if s.pack in names], held, spans, is_last, packs)

    here, there = (0, 1), (1, 0)
    low_swapped, high_swapped = swap(low), swap(high)
    names = [hold(low, (0, 0), here, False), hold(low_swapped, (0, 0), there, False)]
    names += [hold(high, (0, 0), here, True), hold(high_swapped, (0, 0), there, True)]
    if size == 8:
        a = both_links(low)
        b = both_links(low_swapped)
        c = both_links(high)
        sums = run(names, None)
        a, high_swapped, sums = lax.optimization_barrier((a, high_swapped, sums))
        e = both_links(a)
        d = both_links(high_swapped)
        direct, crossed = (4, 2), (2, 4)
        names = [hold(a, direct, there, False), hold(swap(a), crossed, here, False)]
        names += [hold(b, direct, here, False), hold(swap(b), crossed, there, False)]
        sums = run(names, sums)
        c, sums = lax.optimization_barrier((c, sums))
        f = both_links(c)
        names = [hold(c, direct, there, True), hold(swap(c), crossed, here, True)]
        names += [hold(e, (6, 6), here, False), hold(swap(e), (6, 6), there, False)]
        sums = run(names, sums)
        names = [hold(d, direct, here, True), hold(swap(d), crossed, there, True)]
        sums = run(names, sums)
        f, sums = lax.optimization_barrier((f, sums))
        names = [hold(f, (6, 6), here, True), hold(swap(f), (6, 6), there, True)]
        return run(names, sums, True)
    sums = run(names, None)
    for later, block in ((False, low), (True, high)):
        got = {0: block}
        for offset in range(2, size, 2):
            step = offset & -offset
            got[offset] = swap(got[offset ^ step], step)
            names = [hold(got[offset], (offset, offset), here, later)]
            names += [hold(swap(got[offset]), (offset, offset), there, later)]
            sums = run(names, sums, later and offset == size - 2)
    return sums


def solution(mesh):
    in_specs = (P(("dp", "ctx"), None), P(("dp", "ctx"), None, None), P("dp"), P("dp"))
    out_specs = P(("dp", "ctx"), None)
    return jax.shard_map(shards, mesh=mesh, in_specs=in_specs, out_specs=out_specs, check_vma=False)
```

time: 211 us -> 203 us (0.962); the launches traced: 210 us -> 199 us
  Pallas kernels: 0 us -> 163 us
  waiting for transfers between devices: 101 us -> 17.6 us
  matrix products: 45.3 us -> 0 us
  local copies, waits for them, and re-layouts: 32.8 us -> 4.47 us
  other arithmetic: 29.4 us -> 1.59 us
  starting transfers between devices: 0.02 us -> 10.5 us
    pallas_call x0 -> x5, Pallas kernels: none -> 163 us  [run_stage(): pl.pallas_call(functools.partial(stage, held, everything, len(names), spa...]
    ppermute x7 -> x14, waiting for transfers between devices: 101 us -> 17.6 us  [the longest x6 16 us: both_links(): lax.ppermute(block, 'ctx', [(i, i ^ (3 if i % 2 == 0 else 5)) for i in ra...]
    dot_general x16 -> x0, matrix products: 45.3 us -> none  [the longest x8 31.4 us: absorb(): jnp.einsum('qgjk,kgd->qgjd', weights.astype(jnp.bfloat16), value_block, p...]
    reduce_sum x16 -> x1, other arithmetic: 18.6 us -> 0.67 us  [shards(): jnp.sum(jnp.where(jnp.arange(size) == me, halves[:, 0] > halves[:, 1], Fa...]
    while x42 -> x0, local copies, waits for them, and re-layouts: 15.7 us -> none
    ppermute x7 -> x14, starting transfers between devices: 0.02 us -> 10.5 us  [the longest x6 7.06 us: both_links(): lax.ppermute(block, 'ctx', [(i, i ^ (3 if i % 2 == 0 else 5)) for i in ra...]
    unnamed x9 -> x4, local copies, waits for them, and re-layouts: 9.53 us -> 1.82 us
    lt x8 -> x0, other arithmetic: 4.63 us -> none  [the longest x7 4.61 us: absorb(): key_pos < length]
  transfers between devices with their start and end apart: 7 -> 14, of which waited for: 7 -> 8; matrix products, arithmetic and copies ran while one was open for 3% -> 0% of each run, Pallas kernels for 0% -> 6%
where the time goes in v1:
time: 203 us; the launch traced here: 199 us
  Pallas kernels  163 us (80%)
  waiting for transfers between devices  17.6 us (9%)
  starting transfers between devices  10.5 us (5%)
  local copies, waits for them, and re-layouts  4.47 us (2%)
  between operations  2.18 us (1%)
    pallas_call x5, Pallas kernels, run_stage(): pl.pallas_call(functools.partial(stage, held, everything, len(names), spa...  163 us
    ppermute x6, waiting for transfers between devices, both_links(): lax.ppermute(block, 'ctx', [(i, i ^ (3 if i % 2 == 0 else 5)) for i in ra...  16 us
    ppermute x6, starting transfers between devices, both_links(): lax.ppermute(block, 'ctx', [(i, i ^ (3 if i % 2 == 0 else 5)) for i in ra...  7.06 us
  transfers between devices with their start and end apart: 14, of which 8 were waited for; matrix products, arithmetic and copies ran while one was open for 0% of the time, Pallas kernels for 6%

profile of v1, /device:TPU:12, one launch (start us, length us, event | category | flops | bytes accessed | tf_op | source)
XLA Modules:
  0.0 199.2 jit_solution(14495863407816266539)
XLA Ops:
  0.0 0.7 reshape.4
  0.7 0.2 fusion
  0.9 0.7 fusion.1
  2.9 1.9 constant_dynamic-slice_fusion
  4.8 0.1 copy.16
  4.9 0.1 collective-permute-start.3
  5.0 0.1 copy.17
  5.1 0.6 collective-permute-start.2
  5.7 1.2 collective-permute-start.1
  6.8 0.1 collective-permute-done.3.refs_3_.refs_6_
  6.9 1.2 collective-permute-start.5
  8.8 0.7 pad_add_fusion.refs_0_
  9.5 0.0 collective-permute-done.2.refs_5_.refs_8_
  9.5 0.0 copy-start
  9.5 1.6 copy-done
  11.1 2.4 %stage.5.refs_6_ = f32[2,8,512,256]{3,2,1,0:T(8,128)S(1)} custom-call(s32[18]{0:T(128)S(1)} %pad_add_fusion.refs_0_, bf16[256,4096]{1,0:T(8,128)(2,1)S(1)} %copy-done, bf16[1,2,128,1024]{3,2,1,0:T(8,128)(2,1)S(1)} %bitcast.13, bf16[1,2,128,1024]{3,2,1,0:T(8,128)(2,1)S(1)} %collective-permute-done.3.refs_3_.refs_6_, bf16[1,2,128,1024]{3,2,1,0:T(8,128)(2,1)S(1)} %bitcast.16, ...), custom_call_target="tpu_custom_call" | custom-call | flops 2147483648 | bytes 4194304 | tf_op jit(solution)/shard_map/stage/pallas_call | solution.py:220
  13.6 0.7 collective-permute-done.1.refs_2_.refs_9_
  14.3 1.5 collective-permute-start.11
  15.7 1.2 collective-permute-start.4
  17.0 2.9 %collective-permute-done.5.refs_4_.refs_11_ = bf16[1,2,128,1024]{3,2,1,0:T(8,128)(2,1)S(1)} collective-permute-done((bf16[1,2,128,1024]{3,2,1,0:T(8,128)(2,1)S(1)}, bf16[1,2,128,1024]{3,2,1,0:T(8,128)(2,1)S(1)}, u32[]{:S(2)}, u32[]{:S(2)}) %collective-permute-start.5) | collective-permute-done | bytes 524320 | tf_op jit(solution)/shard_map/ppermute | solution.py:247
  19.9 0.4 collective-permute-start.6
  20.3 1.2 collective-permute-start
  21.5 0.5 collective-permute-start.8
  22.0 3.5 %collective-permute-done.11.refs_4_.refs_15_ = bf16[1,2,128,1024]{3,2,1,0:T(8,128)(2,1)S(1)} collective-permute-done((bf16[1,2,128,1024]{3,2,1,0:T(8,128)(2,1)S(1)}, bf16[1,2,128,1024]{3,2,1,0:T(8,128)(2,1)S(1)}, u32[]{:S(2)}, u32[]{:S(2)}) %collective-permute-start.11) | collective-permute-done | bytes 524320 | tf_op jit(solution)/shard_map/ppermute | solution.py:247
  25.5 0.4 collective-permute-start.12
  25.9 0.0 collective-permute-done.4.refs_3_.refs_10_
  25.9 0.0 collective-permute-done.6.refs_5_.refs_12_
  25.9 3.6 %stage.6.refs_6_ = f32[2,8,512,256]{3,2,1,0:T(8,128)S(1)} custom-call(s32[18]{0:T(128)S(1)} %pad_add_fusion.refs_0_, bf16[256,4096]{1,0:T(8,128)(2,1)S(1)} %copy-done, bf16[1,2,128,1024]{3,2,1,0:T(8,128)(2,1)S(1)} %collective-permute-done.1.refs_2_.refs_9_, ...), custom_call_target="tpu_custom_call", output_to_operand_aliasing={{}: (6, {})} | custom-call | flops 2147483648 | bytes 4194304 | tf_op jit(solution)/shard_map/stage/pallas_call | solution.py:220
  29.5 1.7 collective-permute-done.refs_2_.refs_13_
  31.1 0.4 collective-permute-start.10
  31.5 5.3 %collective-permute-done.8.refs_2_.refs_17_ = bf16[1,2,128,1024]{3,2,1,0:T(8,128)(2,1)S(1)} collective-permute-done((bf16[1,2,128,1024]{3,2,1,0:T(8,128)(2,1)S(1)}, bf16[1,2,128,1024]{3,2,1,0:T(8,128)(2,1)S(1)}, u32[]{:S(2)}, u32[]{:S(2)}) %collective-permute-start.8) | collective-permute-done | bytes 524320 | tf_op jit(solution)/shard_map/ppermute | solution.py:247
  36.8 0.1 collective-permute-start.9
  36.9 1.5 collective-permute-start.7
  38.4 0.0 collective-permute-done.12.refs_5_.refs_16_
  38.4 0.0 collective-permute-done.10.refs_3_.refs_14_
  38.4 2.6 %stage.7.refs_4_ = f32[2,8,512,256]{3,2,1,0:T(8,128)S(1)} custom-call(s32[18]{0:T(128)S(1)} %pad_add_fusion.refs_0_, bf16[256,4096]{1,0:T(8,128)(2,1)S(1)} %copy-done, bf16[1,2,128,1024]{3,2,1,0:T(8,128)(2,1)S(1)} %collective-permute-done.refs_2_.refs_13_, ...), custom_call_target="tpu_custom_call", output_to_operand_aliasing={{}: (6, {})} | custom-call | flops 2147483648 | bytes 4194304 | tf_op jit(solution)/shard_map/stage/pallas_call | solution.py:220
  41.0 0.0 collective-permute-done.9.refs_3_.refs_18_
  41.0 2.6 %stage.8.refs_4_ = f32[2,8,512,256]{3,2,1,0:T(8,128)S(1)} custom-call(s32[18]{0:T(128)S(1)} %pad_add_fusion.refs_0_, bf16[256,4096]{1,0:T(8,128)(2,1)S(1)} %copy-done, bf16[1,2,128,1024]{3,2,1,0:T(8,128)(2,1)S(1)} %collective-permute-done.8.refs_2_.refs_17_, ...), custom_call_target="tpu_custom_call", output_to_operand_aliasing={{}: (4, {})} | custom-call | flops 1073741824 | bytes 2097152 | tf_op jit(solution)/shard_map/stage/pallas_call | solution.py:220
  43.6 1.9 collective-permute-done.7.refs_2_.refs_19_
  45.5 0.4 collective-permute-start.13
  45.9 1.5 collective-permute-done.13.refs_3_.refs_20_
  47.4 151.6 %stage.9 = bf16[256,4096]{1,0:T(8,128)(2,1)} custom-call(s32[18]{0:T(128)S(1)} %pad_add_fusion.refs_0_, bf16[256,4096]{1,0:T(8,128)(2,1)S(1)} %copy-done, bf16[1,2,128,1024]{3,2,1,0:T(8,128)(2,1)S(1)} %collective-permute-done.7.refs_2_.refs_19_, bf16[1,2,128,1024]{3,2,1,0:T(8,128)(2,1)S(1)} %collective-permute-done.13.refs_3_.refs_20_, ...), custom_call_target="tpu_custom_call" | custom-call | flops 1073741824 | bytes 2097152 | tf_op jit(solution)/shard_map/stage/pallas_call | solution.py:220
Async XLA Ops:
  4.9 2.0 collective-permute-start.3
  5.1 4.4 %collective-permute-start.2 = (bf16[1,2,128,1024]{3,2,1,0:T(8,128)(2,1)S(1)}, bf16[1,2,128,1024]{3,2,1,0:T(8,128)(2,1)S(1)}, u32[]{:S(2)}, u32[]{:S(2)}) collective-permute-start(bf16[1,2,128,1024]{3,2,1,0:T(8,128)(2,1)S(1)} %bitcast.15), channel_id=1, source_target_pairs={{0,1},{1,0},{2,3},{3,2},{4,5},{5,4},{6,7},{7,6},{8,9},{9,8},{10,11... | collective-permute-start | bytes 1572872 | tf_op jit(solution)/shard_map/ppermute | solution.py:244
  5.7 8.6 %collective-permute-start.1 = (bf16[1,2,128,1024]{3,2,1,0:T(8,128)(2,1)S(1)}, bf16[1,2,128,1024]{3,2,1,0:T(8,128)(2,1)S(1)}, u32[]{:S(2)}, u32[]{:S(2)}) collective-permute-start(bf16[1,2,128,1024]{3,2,1,0:T(8,128)(2,1)S(1)} %bitcast.12), channel_id=1, source_target_pairs={{0,3},{1,4},{2,1},{3,6},{4,7},{5,0},{6,5},{7,2},{8,11},{9,12},{10,... | collective-permute-start | bytes 1572872 | tf_op jit(solution)/shard_map/ppermute | solution.py:247
  6.9 13.0 %collective-permute-start.5 = (bf16[1,2,128,1024]{3,2,1,0:T(8,128)(2,1)S(1)}, bf16[1,2,128,1024]{3,2,1,0:T(8,128)(2,1)S(1)}, u32[]{:S(2)}, u32[]{:S(2)}) collective-permute-start(bf16[1,2,128,1024]{3,2,1,0:T(8,128)(2,1)S(1)} %collective-permute-done.3.refs_3_.refs_6_), channel_id=1, source_target_pairs={{0,3},{1,4},{2,1},{3,6},{4,7},{5,0},{6,5},{7,2},{8,11},{9,12},{10,... | collective-permute-start | bytes 1572872 | tf_op jit(solution)/shard_map/ppermute | solution.py:247
  9.5 1.6 copy-start
  14.3 11.2 %collective-permute-start.11 = (bf16[1,2,128,1024]{3,2,1,0:T(8,128)(2,1)S(1)}, bf16[1,2,128,1024]{3,2,1,0:T(8,128)(2,1)S(1)}, u32[]{:S(2)}, u32[]{:S(2)}) collective-permute-start(bf16[1,2,128,1024]{3,2,1,0:T(8,128)(2,1)S(1)} %collective-permute-done.1.refs_2_.refs_9_), channel_id=1, source_target_pairs={{0,3},{1,4},{2,1},{3,6},{4,7},{5,0},{6,5},{7,2},{8,11},{9,12},{10,... | collective-permute-start | bytes 1572872 | tf_op jit(solution)/shard_map/ppermute | solution.py:247
  15.7 10.1 %collective-permute-start.4 = (bf16[1,2,128,1024]{3,2,1,0:T(8,128)(2,1)S(1)}, bf16[1,2,128,1024]{3,2,1,0:T(8,128)(2,1)S(1)}, u32[]{:S(2)}, u32[]{:S(2)}) collective-permute-start(bf16[1,2,128,1024]{3,2,1,0:T(8,128)(2,1)S(1)} %collective-permute-done.1.refs_2_.refs_9_), channel_id=1, source_target_pairs={{0,1},{1,0},{2,3},{3,2},{4,5},{5,4},{6,7},{7,6},{8,9},{9,8},{10,11... | collective-permute-start | bytes 1572872 | tf_op jit(solution)/shard_map/ppermute | solution.py:244
  19.9 6.0 %collective-permute-start.6 = (bf16[1,2,128,1024]{3,2,1,0:T(8,128)(2,1)S(1)}, bf16[1,2,128,1024]{3,2,1,0:T(8,128)(2,1)S(1)}, u32[]{:S(2)}, u32[]{:S(2)}) collective-permute-start(bf16[1,2,128,1024]{3,2,1,0:T(8,128)(2,1)S(1)} %collective-permute-done.5.refs_4_.refs_11_), channel_id=1, source_target_pairs={{0,1},{1,0},{2,3},{3,2},{4,5},{5,4},{6,7},{7,6},{8,9},{9,8},{10,11... | collective-permute-start | bytes 1572872 | tf_op jit(solution)/shard_map/ppermute | solution.py:244
  20.3 10.9 %collective-permute-start = (bf16[1,2,128,1024]{3,2,1,0:T(8,128)(2,1)S(1)}, bf16[1,2,128,1024]{3,2,1,0:T(8,128)(2,1)S(1)}, u32[]{:S(2)}, u32[]{:S(2)}) collective-permute-start(bf16[1,2,128,1024]{3,2,1,0:T(8,128)(2,1)S(1)} %bitcast.17), channel_id=1, source_target_pairs={{0,3},{1,4},{2,1},{3,6},{4,7},{5,0},{6,5},{7,2},{8,11},{9,12},{10,... | collective-permute-start | bytes 1572872 | tf_op jit(solution)/shard_map/ppermute | solution.py:247
  21.5 15.2 %collective-permute-start.8 = (bf16[1,2,128,1024]{3,2,1,0:T(8,128)(2,1)S(1)}, bf16[1,2,128,1024]{3,2,1,0:T(8,128)(2,1)S(1)}, u32[]{:S(2)}, u32[]{:S(2)}) collective-permute-start(bf16[1,2,128,1024]{3,2,1,0:T(8,128)(2,1)S(1)} %collective-permute-done.2.refs_5_.refs_8_), channel_id=1, source_target_pairs={{0,3},{1,4},{2,1},{3,6},{4,7},{5,0},{6,5},{7,2},{8,11},{9,12},{10,... | collective-permute-start | bytes 1572872 | tf_op jit(solution)/shard_map/ppermute | solution.py:247
  25.5 12.8 %collective-permute-start.12 = (bf16[1,2,128,1024]{3,2,1,0:T(8,128)(2,1)S(1)}, bf16[1,2,128,1024]{3,2,1,0:T(8,128)(2,1)S(1)}, u32[]{:S(2)}, u32[]{:S(2)}) collective-permute-start(bf16[1,2,128,1024]{3,2,1,0:T(8,128)(2,1)S(1)} %collective-permute-done.11.refs_4_.refs_15_), channel_id=1, source_target_pairs={{0,1},{1,0},{2,3},{3,2},{4,5},{5,4},{6,7},{7,6},{8,9},{9,8},{10,11... | collective-permute-start | bytes 1572872 | tf_op jit(solution)/shard_map/ppermute | solution.py:244
  31.1 7.2 %collective-permute-start.10 = (bf16[1,2,128,1024]{3,2,1,0:T(8,128)(2,1)S(1)}, bf16[1,2,128,1024]{3,2,1,0:T(8,128)(2,1)S(1)}, u32[]{:S(2)}, u32[]{:S(2)}) collective-permute-start(bf16[1,2,128,1024]{3,2,1,0:T(8,128)(2,1)S(1)} %collective-permute-done.refs_2_.refs_13_), channel_id=1, source_target_pairs={{0,1},{1,0},{2,3},{3,2},{4,5},{5,4},{6,7},{7,6},{8,9},{9,8},{10,11... | collective-permute-start | bytes 1572872 | tf_op jit(solution)/shard_map/ppermute | solution.py:244
  36.8 4.2 %collective-permute-start.9 = (bf16[1,2,128,1024]{3,2,1,0:T(8,128)(2,1)S(1)}, bf16[1,2,128,1024]{3,2,1,0:T(8,128)(2,1)S(1)}, u32[]{:S(2)}, u32[]{:S(2)}) collective-permute-start(bf16[1,2,128,1024]{3,2,1,0:T(8,128)(2,1)S(1)} %collective-permute-done.8.refs_2_.refs_17_), channel_id=1, source_target_pairs={{0,1},{1,0},{2,3},{3,2},{4,5},{5,4},{6,7},{7,6},{8,9},{9,8},{10,11... | collective-permute-start | bytes 1572872 | tf_op jit(solution)/shard_map/ppermute | solution.py:244
  36.9 8.6 %collective-permute-start.7 = (bf16[1,2,128,1024]{3,2,1,0:T(8,128)(2,1)S(1)}, bf16[1,2,128,1024]{3,2,1,0:T(8,128)(2,1)S(1)}, u32[]{:S(2)}, u32[]{:S(2)}) collective-permute-start(bf16[1,2,128,1024]{3,2,1,0:T(8,128)(2,1)S(1)} %collective-permute-done.refs_2_.refs_13_), channel_id=1, source_target_pairs={{0,3},{1,4},{2,1},{3,6},{4,7},{5,0},{6,5},{7,2},{8,11},{9,12},{10,... | collective-permute-start | bytes 1572872 | tf_op jit(solution)/shard_map/ppermute | solution.py:247
  45.5 1.9 collective-permute-start.13
